TPU v7x, 512 devices: a whole 4x4x16 slice. The times are simulated.
512 devices in a mesh: ctx: 32 (over y_hi, z), tp: 16 (over y_lo, x, core).
Axes of the slice: x: 4, y: 4 (y_hi: 2, y_lo: 2; y = y_hi * 2 + y_lo), z: 16, core: 2. Of those that a mesh axis runs over, the one named last changes fastest.
Arguments:
- query_rows: bfloat16 [4096, 1024], P('ctx', 'tp'), may hold values from -12 to 12
- key_rows: bfloat16 [4096, 1024], P('ctx', 'tp'), may hold values from -6 to 6
- value_rows: bfloat16 [4096, 1024], P('ctx', 'tp'), may hold values from -6 to 6
- valid_frames: int32 [1], replicated, may hold values from 3072 to 4096
- depth_kernel: float32 [32, 1024], P(None, 'tp'), may hold values from -1 to 1
- mix_weight: bfloat16 [1024, 1536], P('tp'), may hold values from -0.1875 to 0.1875
- out_grad: bfloat16 [4096, 1536], P(('ctx', 'tp')), may hold values from -6 to 6
Outputs:
- block_out: bfloat16 [4096, 1536], P(('ctx', 'tp'))
- query_grad: bfloat16 [4096, 1024], P('ctx', 'tp')
- key_grad: bfloat16 [4096, 1024], P('ctx', 'tp')
- value_grad: bfloat16 [4096, 1024], P('ctx', 'tp')
- mix_grad: float32 [1024, 1536], P('tp')
- kernel_grad: float32 [32, 1024], P(None, 'tp')
Inputs may be any that keep to these rules, and one draw needn't show every extreme that they name: Frames from valid_frames on are padding.
All inputs are finite; a program needn't handle non-finite values.
Results may differ from a plain program's by a relative error of at most 0.039.
Values may be sent and summed in bfloat16 or wider, within the bound.
No kernel may reach another device: no remote copies, remote signals or barrier semaphores. Data moves between devices by JAX's collectives and lax.ppermute only.
A program may use at most 64 MiB of HBM per device.

v0:
```python
import jax
import jax.numpy as jnp
from jax import lax
from jax.sharding import PartitionSpec as P

KSIZE = 32


def with_halo(block, sides, width):
    for axis, dim in sides:
        count = lax.axis_size(axis)
        forward = [(i, i + 1) for i in range(count - 1)]
        backward = [(target, source) for source, target in forward]
        low = lax.ppermute(
            lax.slice_in_dim(block, block.shape[dim] - width, None, axis=dim), axis, forward
        )
        high = lax.ppermute(lax.slice_in_dim(block, 0, width, axis=dim), axis, backward)
        block = jnp.concatenate([low, block, high], axis=dim)
    return block


def body(query_rows, key_rows, value_rows, valid_frames, depth_kernel, mix_weight, out_grad):
    frames_dev = query_rows.shape[0]
    head_width = query_rows.shape[1]
    score_scale = head_width ** (-0.5)
    total_frames = frames_dev * lax.axis_size("ctx")
    grad_norm = total_frames ** (-0.5)
    valid_count = valid_frames[0]
    own_ids = lax.axis_index("ctx") * frames_dev + jnp.arange(frames_dev, dtype=jnp.int32)
    own_live = own_ids < valid_count
    key_value = jnp.concatenate([key_rows, value_rows], axis=1)
    contract_last = (((1,), (1,)), ((), ()))
    key_piece = lax.all_gather(key_rows, "ctx", axis=0, tiled=True)
    run_max = jnp.full((frames_dev,), -1e30, jnp.float32)
    key_part = key_piece
    key_live = jnp.arange(key_piece.shape[0], dtype=jnp.int32) < valid_count
    scores = score_scale * lax.dot_general(
        query_rows, key_part, contract_last, preferred_element_type=jnp.float32
    )
    capped = jnp.where(key_live[None, :], scores, -1e30)
    new_max = jnp.maximum(run_max, jnp.max(capped, axis=1))
    weights = jnp.where(key_live[None, :], jnp.exp(capped - new_max[:, None]), 0.0)
    run_total = jnp.sum(weights, axis=1)
    run_max, run_total = (new_max, run_total)
    log_total = run_max + jnp.log(run_total)
    key_piece = lax.all_gather(key_value, "ctx", axis=0, tiled=True)
    key_part = key_piece[:, :head_width]
    value_part = key_piece[:, head_width:]
    key_live = jnp.arange(key_piece.shape[0], dtype=jnp.int32) < valid_count
    scores = score_scale * lax.dot_general(
        query_rows, key_part, contract_last, preferred_element_type=jnp.float32
    )
    capped = jnp.where(key_live[None, :], scores, -1e30)
    probs = jnp.where(key_live[None, :], jnp.exp(capped - log_total[:, None]), 0.0).astype(
        jnp.bfloat16
    )
    run_out = jnp.dot(probs, value_part, preferred_element_type=jnp.float32)
    attn = run_out.astype(jnp.bfloat16)
    masked = jnp.where(own_live[:, None], attn, jnp.zeros_like(attn))
    rim_width = KSIZE // 2
    padded_attn = with_halo(masked, (("ctx", 0),), rim_width)
    depth_out = jnp.zeros((frames_dev, head_width), jnp.float32)
    for offset in range(KSIZE):
        depth_out = depth_out + depth_kernel[offset][None, :] * padded_attn[
            offset : offset + frames_dev
        ].astype(jnp.float32)
    swished = (depth_out * jax.nn.sigmoid(depth_out)).astype(jnp.bfloat16)
    channel_rows = lax.all_to_all(swished, "tp", split_axis=0, concat_axis=1, tiled=True)
    full_weight = lax.all_gather(mix_weight, "tp", axis=0, tiled=True)
    block_out = jnp.dot(channel_rows, full_weight, preferred_element_type=jnp.float32).astype(
        jnp.bfloat16
    )
    grad_block = lax.all_gather(out_grad, "tp", axis=0, tiled=True)
    mix_back = lax.dot_general(
        grad_block, mix_weight, contract_last, preferred_element_type=jnp.float32
    )
    gate_sig = jax.nn.sigmoid(depth_out)
    depth_grad = (mix_back * gate_sig * (1.0 + depth_out * (1.0 - gate_sig))).astype(jnp.bfloat16)
    mix_part = lax.dot_general(
        swished, grad_block, (((0,), (0,)), ((), ())), preferred_element_type=jnp.float32
    )
    depth_grad_wide = depth_grad.astype(jnp.float32)
    kernel_rows = []
    for offset in range(KSIZE):
        kernel_rows.append(
            jnp.sum(
                padded_attn[offset : offset + frames_dev].astype(jnp.float32) * depth_grad_wide,
                axis=0,
            )
        )
    kernel_part = jnp.stack(kernel_rows, axis=0)
    mix_total, kernel_total = (
        lax.psum(mix_part.astype(jnp.bfloat16), "ctx").astype(jnp.float32),
        lax.psum(kernel_part.astype(jnp.bfloat16), "ctx").astype(jnp.float32),
    )
    mix_grad = grad_norm * mix_total
    kernel_grad = grad_norm * kernel_total
    padded_grad = with_halo(depth_grad, (("ctx", 0),), rim_width)
    back_sum = jnp.zeros((frames_dev, head_width), jnp.float32)
    for offset in range(KSIZE):
        first_row = 2 * rim_width - offset
        back_sum = back_sum + depth_kernel[offset][None, :] * padded_grad[
            first_row : first_row + frames_dev
        ].astype(jnp.float32)
    attn_grad = jnp.where(own_live[:, None], back_sum, jnp.zeros_like(back_sum)).astype(
        jnp.bfloat16
    )
    delta = jnp.sum(attn_grad.astype(jnp.float32) * attn.astype(jnp.float32), axis=1)
    key_piece = lax.all_gather(key_value, "ctx", axis=0, tiled=True)
    key_part = key_piece[:, :head_width]
    value_part = key_piece[:, head_width:]
    key_live = jnp.arange(key_piece.shape[0], dtype=jnp.int32) < valid_count
    scores = score_scale * lax.dot_general(
        query_rows, key_part, contract_last, preferred_element_type=jnp.float32
    )
    capped = jnp.where(key_live[None, :], scores, -1e30)
    weights = jnp.where(key_live[None, :], jnp.exp(capped - log_total[:, None]), 0.0)
    dprobs = lax.dot_general(
        attn_grad, value_part, contract_last, preferred_element_type=jnp.float32
    )
    dscores = (weights * (dprobs - delta[:, None])).astype(jnp.bfloat16)
    query_total = score_scale * jnp.dot(dscores, key_part, preferred_element_type=jnp.float32)
    query_grad = query_total.astype(jnp.bfloat16)
    query_and_grad = jnp.concatenate([query_rows, attn_grad], axis=1)
    row_stats = jnp.stack([log_total, delta], axis=1)
    all_stats = lax.all_gather(row_stats, "ctx", axis=0, tiled=True)
    rows_piece = lax.all_gather(query_and_grad, "ctx", axis=0, tiled=True)
    query_piece = rows_piece[:, :head_width]
    grad_piece = rows_piece[:, head_width:]
    total_piece = all_stats[:, 0]
    delta_piece = all_stats[:, 1]
    scores = score_scale * lax.dot_general(
        key_rows, query_piece, contract_last, preferred_element_type=jnp.float32
    )
    capped = jnp.where(own_live[:, None], scores, -1e30)
    weights = jnp.where(own_live[:, None], jnp.exp(capped - total_piece[None, :]), 0.0)
    dprobs = lax.dot_general(
        value_rows, grad_piece, contract_last, preferred_element_type=jnp.float32
    )
    dscores = (weights * (dprobs - delta_piece[None, :])).astype(jnp.bfloat16)
    key_total = score_scale * jnp.dot(dscores, query_piece, preferred_element_type=jnp.float32)
    value_total = jnp.dot(
        weights.astype(jnp.bfloat16), grad_piece, preferred_element_type=jnp.float32
    )
    key_total, value_total = (key_total, value_total)
    return (
        block_out,
        query_grad,
        key_total.astype(jnp.bfloat16),
        value_total.astype(jnp.bfloat16),
        mix_grad,
        kernel_grad,
    )


def solution(mesh):
    placed = (
        P("ctx", "tp"),
        P("ctx", "tp"),
        P("ctx", "tp"),
        P(),
        P(None, "tp"),
        P("tp", None),
        P(("ctx", "tp"), None),
    )
    return jax.shard_map(
        body,
        mesh=mesh,
        in_specs=placed,
        out_specs=(
            P(("ctx", "tp"), None),
            P("ctx", "tp"),
            P("ctx", "tp"),
            P("ctx", "tp"),
            P("tp", None),
            P(None, "tp"),
        ),
        check_vma=False,
    )
```

profile of v0, /device:TPU:1, one launch (start us, length us, event | category | flops | bytes accessed | tf_op | source)
XLA Modules:
  0.0 650.3 jit_solution(8706354773599395544)
XLA Ops:
  7.2 1.4 pad_maximum_fusion
  9.3 72.7 %all_gather.20 = bf16[4096,64]{0,1:T(8,128)(2,1)S(1)} all-gather(bf16[128,64]{0,1:T(8,128)(2,1)} %param.8), channel_id=1, replica_groups=mesh['ctx'=32,'tp'=16] {'ctx'}, dimensions={0}, use_global_device_ids=true | all-gather | bytes 540672 | tf_op jit(solution)/shard_map/all_gather | solution.py:33
  82.1 1.3 fusion.177
  84.0 58.7 %all-gather.4.cloned.1.call-done = bf16[4096,128]{0,1:T(8,128)(2,1)} async-done(((bf16[128,128]{0,1:T(8,128)(2,1)}), bf16[4096,128]{0,1:T(8,128)(2,1)}) %all-gather.4.cloned.1.call-update) | async-done | bytes 1048592 | tf_op jit(solution)/shard_map/all_gather | solution.py:46
  142.7 3.0 fusion.8
  146.1 1.3 collective-permute-start.1
  147.4 4.0 collective-permute-start
  151.4 30.7 %all_gather.22 = bf16[128,1536]{1,0:T(8,128)(2,1)S(1)} all-gather(bf16[8,1536]{1,0:T(8,128)(2,1)S(1)} %copy-done.6), channel_id=1, replica_groups=mesh['ctx'=32,'tp'=16] {'tp'}, dimensions={0}, use_global_device_ids=true | all-gather | bytes 417792 | tf_op jit(solution)/shard_map/all_gather | solution.py:73
  183.3 2.9 collective-permute-start.3
  186.2 1.3 collective-permute-start.2
  187.5 0.9 convolution_convert_fusion
  188.5 2.2 collective-permute-done.2
  193.3 4.9 all-to-all-start
  199.5 62.3 %psum.15 = bf16[32,64]{1,0:T(8,128)(2,1)S(1)} all-reduce(bf16[32,64]{1,0:T(8,128)(2,1)S(1)} %stack.170), channel_id=1, replica_groups=mesh['ctx'=32,'tp'=16] {'ctx'}, use_global_device_ids=true, to_apply=%region_36.37 | all-reduce | flops 2048 | bytes 8192 | tf_op jit(solution)/shard_map/psum | solution.py:94
  262.4 58.0 %all_gather.24 = f32[4096,2]{0,1:T(2,128)S(1)} all-gather(f32[128,2]{0,1:T(2,128)S(1)} %pad_maximum_fusion.6), channel_id=1, replica_groups=mesh['ctx'=32,'tp'=16] {'ctx'}, dimensions={0}, use_global_device_ids=true | all-gather | bytes 33792 | tf_op jit(solution)/shard_map/all_gather | solution.py:126
  320.4 1.4 fusion.21
  322.1 127.2 %all-reduce.2.cloned.1.call-done = bf16[64,1536]{1,0:T(8,128)(2,1)} async-done(((bf16[64,1536]{1,0:T(8,128)(2,1)}), bf16[64,1536]{1,0:T(8,128)(2,1)}) %all-reduce.2.cloned.1.call-update) | async-done | bytes 196624 | tf_op jit(solution)/shard_map/psum | solution.py:93
  449.3 1.7 convert_multiply_fusion
  451.0 139.8 %all-gather.8.cloned.1.call-done = bf16[4096,128]{0,1:T(8,128)(2,1)} async-done(((bf16[128,128]{0,1:T(8,128)(2,1)}), bf16[4096,128]{0,1:T(8,128)(2,1)}) %all-gather.8.cloned.1.call-update) | async-done | bytes 1048592 | tf_op jit(solution)/shard_map/all_gather | solution.py:127
  590.8 2.1 fusion.11
  592.9 0.9 convolution_convert_fusion.2
  593.8 1.7 fusion.20
  595.5 45.2 %all-gather.6.cloned.1.call-done = bf16[1024,1536]{1,0:T(8,128)(2,1)} async-done(((bf16[64,1536]{1,0:T(8,128)(2,1)}), bf16[1024,1536]{1,0:T(8,128)(2,1)}) %all-gather.6.cloned.1.call-update) | async-done | bytes 3145744 | tf_op jit(solution)/shard_map/all_gather | solution.py:69
  640.7 3.0 convolution_convert_fusion.1
  (54 shorter events, 7.0 us)
Async XLA Ops:
  7.2 135.6 %all-gather.4.cloned.1.call-start = ((), (), s32[]{:S(2)}) async-start(), calls=%async_computation.1 | async-start | bytes 1081344 | tf_op jit(solution)/shard_map/all_gather | solution.py:46
  8.6 440.7 %all-reduce.2.cloned.1.call-start = ((), (), s32[]{:S(2)}) async-start(), calls=%async_computation.4 | async-start | bytes 393216 | tf_op jit(solution)/shard_map/psum | solution.py:93
  82.1 1.9 copy-start.7
  82.1 60.7 %copy-start.3 = (bf16[128,64]{0,1:T(8,128)(2,1)S(1)}, bf16[128,64]{0,1:T(8,128)(2,1)}, u32[]{:S(2)}) copy-start(bf16[128,64]{0,1:T(8,128)(2,1)} %param.7) | copy-start | bytes 49156
  142.7 3.0 copy-start.1
  145.7 5.7 copy-start.6
  145.7 37.0 %copy-start.2 = (bf16[64,1536]{1,0:T(8,128)(2,1)S(1)}, bf16[64,1536]{1,0:T(8,128)(2,1)}, u32[]{:S(2)}) copy-start(bf16[64,1536]{1,0:T(8,128)(2,1)} %param.12) | copy-start | bytes 589828
  146.1 36.0 %collective-permute-start.1 = (bf16[16,64]{0,1:T(8,128)(2,1)S(1)}, bf16[16,64]{0,1:T(8,128)(2,1)S(1)}, u32[]{:S(2)}, u32[]{:S(2)}) collective-permute-start(bf16[16,64]{0,1:T(8,128)(2,1)S(1)} %get-tuple-element.79), channel_id=1, source_target_pairs={{16,0},{32,16},{48,32},{64,48},{80,64},{96,80},{112,96},{128,112},... | collective-permute-start | bytes 6152 | tf_op jit(solution)/shard_map/ppermute | solution.py:17
  147.4 34.7 %collective-permute-start = (bf16[16,64]{0,1:T(8,128)(2,1)S(1)}, bf16[16,64]{0,1:T(8,128)(2,1)S(1)}, u32[]{:S(2)}, u32[]{:S(2)}) collective-permute-start(bf16[16,64]{0,1:T(8,128)(2,1)S(1)} %get-tuple-element.78), channel_id=1, source_target_pairs={{0,16},{16,32},{32,48},{48,64},{64,80},{80,96},{96,112},{112,128},... | collective-permute-start | bytes 6152 | tf_op jit(solution)/shard_map/ppermute | solution.py:14
  183.3 5.2 collective-permute-start.3
  186.2 4.5 collective-permute-start.2
  188.4 402.4 %all-gather.8.cloned.1.call-start = ((), (), s32[]{:S(2)}) async-start(), calls=%async_computation.3 | async-start | bytes 1081344 | tf_op jit(solution)/shard_map/all_gather | solution.py:127
  191.9 448.8 %all-gather.6.cloned.1.call-start = ((), (), s32[]{:S(2)}) async-start(), calls=%async_computation.2 | async-start | bytes 3342336 | tf_op jit(solution)/shard_map/all_gather | solution.py:69
  193.3 128.5 %all-to-all-start = ((bf16[16,2,256]{2,1,0:T(2,128)(2,1)}), bf16[16,2,256]{2,1,0:T(2,128)(2,1)S(1)}, u32[]{:S(2)}, u32[]{:S(2)}) async-start(bf16[16,2,256]{2,1,0:T(2,128)(2,1)} %reshape.50), calls=%async_computation | async-start | bytes 32768 | tf_op jit(solution)/shard_map/all_to_all | solution.py:68
  199.3 391.5 %copy-start.5 = (bf16[128,64]{0,1:T(8,128)(2,1)S(1)}, bf16[128,64]{0,1:T(8,128)(2,1)}, u32[]{:S(2)}) copy-start(bf16[128,64]{0,1:T(8,128)(2,1)} %param.8) | copy-start | bytes 49156
  590.8 2.1 copy-start
  592.9 0.9 copy-start.4
Sparse Core Ops, SparseCore 0:
  11.5 131.2 all-gather.3
  188.5 260.7 all-reduce.1
  452.6 138.1 all-gather.7
  593.0 47.6 all-gather.5
where the time goes:
time: 651 us; the launch traced here: 650 us
  waiting for transfers between devices  374 us (57%)
  blocking collectives  224 us (34%)
  matrix products  15 us (2%)
  between operations  14.6 us (2%)
  starting transfers between devices  14.5 us (2%)
  other arithmetic  7.18 us (1%)
    all_gather x1, waiting for transfers between devices, body(): rows_piece = lax.all_gather(query_and_grad, 'ctx', axis=0, tiled=True)  140 us
    psum x1, waiting for transfers between devices, body(): lax.psum(mix_part.astype(jnp.bfloat16), 'ctx').astype(jnp.float32)  127 us
    all_gather x1, blocking collectives, body(): key_piece = lax.all_gather(key_rows, 'ctx', axis=0, tiled=True)  72.7 us
    psum x1, blocking collectives, body(): lax.psum(kernel_part.astype(jnp.bfloat16), 'ctx').astype(jnp.float32)  62.3 us
    all_gather x1, waiting for transfers between devices, body(): key_piece = lax.all_gather(key_value, 'ctx', axis=0, tiled=True)  58.7 us
    all_gather x1, blocking collectives, body(): all_stats = lax.all_gather(row_stats, 'ctx', axis=0, tiled=True)  58 us
    all_gather x1, waiting for transfers between devices, body(): full_weight = lax.all_gather(mix_weight, 'tp', axis=0, tiled=True)  45.2 us
    all_gather x1, blocking collectives, body(): grad_block = lax.all_gather(out_grad, 'tp', axis=0, tiled=True)  30.7 us
  transfers between devices with their start and end apart: 9, of which 5 were waited for; matrix products, arithmetic and copies ran while one was open for 2% of the time, Pallas kernels for 0%

commit v1 on v0

--- a/solution.py
+++ b/solution.py
@@ -124,7 +124,12 @@
     query_and_grad = jnp.concatenate([query_rows, attn_grad], axis=1)
     row_stats = jnp.stack([log_total, delta], axis=1)
     all_stats = lax.all_gather(row_stats, "ctx", axis=0, tiled=True)
-    rows_piece = lax.all_gather(query_and_grad, "ctx", axis=0, tiled=True)
+    rows_piece = jnp.concatenate(
+        lax.all_to_all(
+            jnp.stack([query_and_grad for _ in range(lax.axis_size("ctx"))], axis=0), "ctx", 0, 0
+        ),
+        axis=0,
+    )
     query_piece = rows_piece[:, :head_width]
     grad_piece = rows_piece[:, head_width:]
     total_piece = all_stats[:, 0]

time: 651 us -> 489 us (0.75)
  the two profiles are of different devices: /device:TPU:1 before, /device:TPU:2 now
where the time goes in v1:
time: 489 us
  blocking collectives  289 us (59%)
  waiting for transfers between devices  130 us (27%)
  starting transfers between devices  27.7 us (6%)
  between operations  16.4 us (3%)
  matrix products  16 us (3%)
  other arithmetic  6.6 us (1%)
    psum x1, blocking collectives, body(): lax.psum(kernel_part.astype(jnp.bfloat16), 'ctx').astype(jnp.float32)  115 us
    all_gather x1, blocking collectives, body(): key_piece = lax.all_gather(key_rows, 'ctx', axis=0, tiled=True)  85.7 us
    psum x1, waiting for transfers between devices, body(): lax.psum(mix_part.astype(jnp.bfloat16), 'ctx').astype(jnp.float32)  71 us
    all_gather x1, blocking collectives, body(): all_stats = lax.all_gather(row_stats, 'ctx', axis=0, tiled=True)  70.5 us
    all_gather x1, waiting for transfers between devices, body(): key_piece = lax.all_gather(key_value, 'ctx', axis=0, tiled=True)  54.9 us
    all_gather x1, blocking collectives, body(): grad_block = lax.all_gather(out_grad, 'tp', axis=0, tiled=True)  17.5 us
    all_to_all x1, starting transfers between devices, body(): lax.all_to_all(jnp.stack([query_and_grad for _ in range(lax.axis_size('ct...  11.2 us
  transfers between devices with their start and end apart: 9, of which 3 were waited for; matrix products, arithmetic and copies ran while one was open for 3% of the time, Pallas kernels for 0%

profile of v1, /device:TPU:2, one launch (start us, length us, event | category | flops | bytes accessed | tf_op | source)
XLA Modules:
  0.0 488.8 jit_solution(15760486915014571643)
XLA Ops:
  8.0 1.4 pad_maximum_fusion
  10.1 85.7 %all_gather.17 = bf16[4096,64]{0,1:T(8,128)(2,1)S(1)} all-gather(bf16[128,64]{0,1:T(8,128)(2,1)} %param.8), channel_id=1, replica_groups=mesh['ctx'=32,'tp'=16] {'ctx'}, dimensions={0}, use_global_device_ids=true | all-gather | bytes 540672 | tf_op jit(solution)/shard_map/all_gather | solution.py:33
  95.8 1.3 fusion.177
  97.8 54.9 %all-gather.3.cloned.1.call-done = bf16[4096,128]{0,1:T(8,128)(2,1)} async-done(((bf16[128,128]{0,1:T(8,128)(2,1)}), bf16[4096,128]{0,1:T(8,128)(2,1)}) %all-gather.3.cloned.1.call-update) | async-done | bytes 1048592 | tf_op jit(solution)/shard_map/all_gather | solution.py:46
  152.7 3.0 fusion.11
  156.0 1.3 collective-permute-start.1
  157.3 4.5 collective-permute-start
  161.9 17.5 %all_gather.19 = bf16[128,1536]{1,0:T(8,128)(2,1)S(1)} all-gather(bf16[8,1536]{1,0:T(8,128)(2,1)S(1)} %copy-done.5), channel_id=1, replica_groups=mesh['ctx'=32,'tp'=16] {'tp'}, dimensions={0}, use_global_device_ids=true | all-gather | bytes 417792 | tf_op jit(solution)/shard_map/all_gather | solution.py:73
  180.1 0.9 convolution_convert_fusion
  182.1 3.2 collective-permute-start.3
  185.3 1.3 collective-permute-start.2
  187.4 6.0 %all-to-all-start = ((bf16[16,2,256]{2,1,0:T(2,128)(2,1)}), bf16[16,2,256]{2,1,0:T(2,128)(2,1)S(1)}, u32[]{:S(2)}, u32[]{:S(2)}) async-start(bf16[16,2,256]{2,1,0:T(2,128)(2,1)} %reshape.56), calls=%async_computation | async-start | bytes 32768 | tf_op jit(solution)/shard_map/all_to_all | solution.py:68
  194.2 4.0 all-to-all-done
  198.2 1.2 stack.172
  199.4 11.2 %all-to-all-start.1 = ((bf16[32,128,128]{2,1,0:T(8,128)(2,1)}), bf16[32,128,128]{2,1,0:T(8,128)(2,1)S(1)}, u32[]{:S(2)}, u32[]{:S(2)}) async-start(bf16[32,128,128]{2,1,0:T(8,128)(2,1)} %stack.172), calls=%async_computation.1 | async-start | bytes 2097152 | tf_op jit(solution)/shard_map/all_to_all | solution.py:128
  211.9 115.4 %psum.15 = bf16[32,64]{1,0:T(8,128)(2,1)S(1)} all-reduce(bf16[32,64]{1,0:T(8,128)(2,1)S(1)} %stack.206), channel_id=1, replica_groups=mesh['ctx'=32,'tp'=16] {'ctx'}, use_global_device_ids=true, to_apply=%region_36.37 | all-reduce | flops 2048 | bytes 8192 | tf_op jit(solution)/shard_map/psum | solution.py:94
  327.9 70.5 %all_gather.20 = f32[4096,2]{0,1:T(2,128)S(1)} all-gather(f32[128,2]{0,1:T(2,128)S(1)} %pad_maximum_fusion.6), channel_id=1, replica_groups=mesh['ctx'=32,'tp'=16] {'ctx'}, dimensions={0}, use_global_device_ids=true | all-gather | bytes 33792 | tf_op jit(solution)/shard_map/all_gather | solution.py:126
  398.4 2.6 fusion.20
  401.3 71.0 %all-reduce.2.cloned.1.call-done = bf16[64,1536]{1,0:T(8,128)(2,1)} async-done(((bf16[64,1536]{1,0:T(8,128)(2,1)}), bf16[64,1536]{1,0:T(8,128)(2,1)}) %all-reduce.2.cloned.1.call-update) | async-done | bytes 196624 | tf_op jit(solution)/shard_map/psum | solution.py:93
  472.2 1.7 convert_multiply_fusion
  474.0 3.0 convolution_convert_fusion.1
  477.0 0.8 fusion.4
  477.8 1.6 convolution_convert_fusion.3
  479.4 1.9 fusion.21
  (53 shorter events, 6.5 us)
Async XLA Ops:
  8.0 144.7 %all-gather.3.cloned.1.call-start = ((), (), s32[]{:S(2)}) async-start(), calls=%async_computation.2 | async-start | bytes 1081344 | tf_op jit(solution)/shard_map/all_gather | solution.py:46
  9.4 462.8 %all-reduce.2.cloned.1.call-start = ((), (), s32[]{:S(2)}) async-start(), calls=%async_computation.4 | async-start | bytes 393216 | tf_op jit(solution)/shard_map/psum | solution.py:93
  95.8 1.9 copy-start.6
  95.8 56.8 %copy-start.2 = (bf16[128,64]{0,1:T(8,128)(2,1)S(1)}, bf16[128,64]{0,1:T(8,128)(2,1)}, u32[]{:S(2)}) copy-start(bf16[128,64]{0,1:T(8,128)(2,1)} %param.7) | copy-start | bytes 49156
  152.7 3.0 copy-start
  155.6 6.3 %copy-start.5 = (bf16[8,1536]{1,0:T(8,128)(2,1)S(1)}, bf16[8,1536]{1,0:T(8,128)(2,1)}, u32[]{:S(2)}) copy-start(bf16[8,1536]{1,0:T(8,128)(2,1)} %param.13) | copy-start | bytes 73732
  155.6 25.9 %copy-start.1 = (bf16[64,1536]{1,0:T(8,128)(2,1)S(1)}, bf16[64,1536]{1,0:T(8,128)(2,1)}, u32[]{:S(2)}) copy-start(bf16[64,1536]{1,0:T(8,128)(2,1)} %param.12) | copy-start | bytes 589828
  156.0 23.4 %collective-permute-start.1 = (bf16[16,64]{0,1:T(8,128)(2,1)S(1)}, bf16[16,64]{0,1:T(8,128)(2,1)S(1)}, u32[]{:S(2)}, u32[]{:S(2)}) collective-permute-start(bf16[16,64]{0,1:T(8,128)(2,1)S(1)} %get-tuple-element.79), channel_id=1, source_target_pairs={{16,0},{32,16},{48,32},{64,48},{80,64},{96,80},{112,96},{128,112},... | collective-permute-start | bytes 6152 | tf_op jit(solution)/shard_map/ppermute | solution.py:17
  157.3 22.1 %collective-permute-start = (bf16[16,64]{0,1:T(8,128)(2,1)S(1)}, bf16[16,64]{0,1:T(8,128)(2,1)S(1)}, u32[]{:S(2)}, u32[]{:S(2)}) collective-permute-start(bf16[16,64]{0,1:T(8,128)(2,1)S(1)} %get-tuple-element.78), channel_id=1, source_target_pairs={{0,16},{16,32},{32,48},{48,64},{64,80},{80,96},{96,112},{112,128},... | collective-permute-start | bytes 6152 | tf_op jit(solution)/shard_map/ppermute | solution.py:14
  181.0 293.0 %all-gather.5.cloned.1.call-start = ((), (), s32[]{:S(2)}) async-start(), calls=%async_computation.3 | async-start | bytes 3342336 | tf_op jit(solution)/shard_map/all_gather | solution.py:69
  182.1 11.3 %collective-permute-start.3 = (bf16[16,64]{0,1:T(8,128)(2,1)S(1)}, bf16[16,64]{0,1:T(8,128)(2,1)S(1)}, u32[]{:S(2)}, u32[]{:S(2)}) collective-permute-start(bf16[16,64]{0,1:T(8,128)(2,1)S(1)} %get-tuple-element.45), channel_id=1, source_target_pairs={{0,16},{16,32},{32,48},{48,64},{64,80},{80,96},{96,112},{112,128},... | collective-permute-start | bytes 6152 | tf_op jit(solution)/shard_map/ppermute | solution.py:14
  185.3 8.1 %collective-permute-start.2 = (bf16[16,64]{0,1:T(8,128)(2,1)S(1)}, bf16[16,64]{0,1:T(8,128)(2,1)S(1)}, u32[]{:S(2)}, u32[]{:S(2)}) collective-permute-start(bf16[16,64]{0,1:T(8,128)(2,1)S(1)} %get-tuple-element.44), channel_id=1, source_target_pairs={{16,0},{32,16},{48,32},{64,48},{80,64},{96,80},{112,96},{128,112},... | collective-permute-start | bytes 6152 | tf_op jit(solution)/shard_map/ppermute | solution.py:17
  187.4 10.8 %all-to-all-start = ((bf16[16,2,256]{2,1,0:T(2,128)(2,1)}), bf16[16,2,256]{2,1,0:T(2,128)(2,1)S(1)}, u32[]{:S(2)}, u32[]{:S(2)}) async-start(bf16[16,2,256]{2,1,0:T(2,128)(2,1)} %reshape.56), calls=%async_computation | async-start | bytes 32768 | tf_op jit(solution)/shard_map/all_to_all | solution.py:68
  199.4 277.5 %all-to-all-start.1 = ((bf16[32,128,128]{2,1,0:T(8,128)(2,1)}), bf16[32,128,128]{2,1,0:T(8,128)(2,1)S(1)}, u32[]{:S(2)}, u32[]{:S(2)}) async-start(bf16[32,128,128]{2,1,0:T(8,128)(2,1)} %stack.172), calls=%async_computation.1 | async-start | bytes 2097152 | tf_op jit(solution)/shard_map/all_to_all | solution.py:128
  401.0 76.0 %copy-start.4 = (bf16[128,64]{0,1:T(8,128)(2,1)S(1)}, bf16[128,64]{0,1:T(8,128)(2,1)}, u32[]{:S(2)}) copy-start(bf16[128,64]{0,1:T(8,128)(2,1)} %param.8) | copy-start | bytes 49156
  477.8 1.6 copy-start.3
Sparse Core Ops, SparseCore 0:
  12.3 140.2 all-gather.2
  181.1 291.1 all-reduce.1
Sparse Core Ops, SparseCore 1:
  183.6 39.5 all-gather.4
